TPU v7x, 32 devices: a whole 2x2x4 slice. The times are simulated.
32 devices in a mesh: parts: 2 (over y), tile: 16 (over z, x, core).
Axes of the slice: x: 2, y: 2, z: 4, core: 2. Of those that a mesh axis runs over, the one named last changes fastest.
Arguments:
- density: bfloat16 [512, 256], P(('parts', 'tile')), parts along dimension 0, may hold values from -6 to 6
- three_center: bfloat16 [96, 32, 256, 128], P(('parts', 'tile')), parts along dimension 0, may hold values from -0.125 to 0.125
- metric: float32 [96, 128, 128], P(('parts', 'tile')), parts along dimension 0, may hold values from -1 to 2
- fetch_owner: int32 [11264, 1], P(('parts', 'tile')), parts along dimension 0, may hold values from 0 to 15; in each aligned block of 352 rows (0 to 351, 352 to 703, ...) at most 35 rows name the same one
- fetch_slot: int32 [11264], P(('parts', 'tile')), parts along dimension 0, may hold values from 0 to 15
- basis_value: bfloat16 [128, 32, 16, 128], P(('parts', 'tile')), parts along dimension 0, may hold values from -1 to 1
- basis_gradient: bfloat16 [128, 32, 3, 16, 128], P(('parts', 'tile')), parts along dimension 0, may hold values from -4 to 4
- pair_slot: int32 [128, 64, 2], P(('parts', 'tile')), parts along dimension 0, may hold values from 0 to 31
- base_density: float32 [128, 128], P(('parts', 'tile')), parts along dimension 0, may hold values from 0.3 to 3
- base_kinetic: float32 [128, 128], P(('parts', 'tile')), parts along dimension 0, may hold values from 4 to 40
- grid_weight: float32 [128, 128], P(('parts', 'tile')), parts along dimension 0, may hold values from 1 to 4
Outputs:
- coulomb: float32 [512, 256], P(('parts', 'tile')), parts along dimension 0
- exchange_corr: float32 [512, 256], P(('parts', 'tile')), parts along dimension 0
There are 2 independent parts, one for each index of `parts`. A program takes and returns all parts, laid end to end along the dimension named above; each array names one. Nothing has to cross between parts.
Inputs may be any that keep to these rules, and one draw needn't show every extreme that they name: `fetch_owner`: in each of the 16 lists of 352 references, no owner is named more than 35 times, and in some list one owner is named exactly 35 times.
All inputs are finite; a program needn't handle non-finite values.
Results may differ from a plain program's by a relative error of at most 0.0049.
Values may be sent and summed in bfloat16 or wider, within the bound.
A program may use at most 64 MiB of HBM per device.

v0:
```python
import jax
import jax.numpy as jnp
from jax import lax
from jax.sharding import PartitionSpec as P

CX_COEF = 0.7385587663820224
CS_COEF = 0.026121172985233605
CTF_COEF = 2.871234000188191
KAPPA_VALUE = 0.804
MU_COEF = 0.12345679012345678
H_ZERO = 1.174


def smooth_floor(amount):
    return 0.5 * (amount + jnp.sqrt(amount * amount + 1.0))


def point_energy(dens_point, grad_square, kinetic):
    s_square = CS_COEF * grad_square / jnp.power(dens_point, 8.0 / 3.0)
    h_one = 1.0 + KAPPA_VALUE - KAPPA_VALUE / (1.0 + MU_COEF * s_square / KAPPA_VALUE)
    iso_alpha = (kinetic - grad_square / (8.0 * dens_point)) / (
        CTF_COEF * jnp.power(dens_point, 5.0 / 3.0)
    )
    factor = h_one + (H_ZERO - h_one) / (1.0 + iso_alpha * iso_alpha)
    return -CX_COEF * jnp.power(dens_point, 4.0 / 3.0) * factor


def batch_potential(inputs):
    point_value, point_slope, slot_pairs, tile_rows, base_rho, base_tau, weights = inputs
    basis = jnp.concatenate([point_value[:, None], point_slope], axis=1).astype(jnp.float32)
    left_basis = basis[slot_pairs[:, 0]]
    right_basis = basis[slot_pairs[:, 1]]
    count = tile_rows.shape[0]
    tile_edge = basis.shape[2]
    start = tile_rows.astype(jnp.float32).reshape(count, tile_edge, tile_edge)

    def energy(tile_values):
        mixed_terms = jnp.einsum("rmn,rcng->rcmg", tile_values, right_basis)
        point_rho = jnp.sum(left_basis[:, 0] * mixed_terms[:, 0], axis=(0, 1))
        point_grad = jnp.sum(
            left_basis[:, 1:] * mixed_terms[:, :1] + left_basis[:, :1] * mixed_terms[:, 1:],
            axis=(0, 2),
        )
        point_tau = 0.5 * jnp.sum(left_basis[:, 1:] * mixed_terms[:, 1:], axis=(0, 1, 2))
        dens_point = smooth_floor(base_rho + point_rho)
        kinetic = smooth_floor(base_tau + point_tau)
        grad_square = jnp.sum(point_grad * point_grad, axis=0)
        return jnp.sum(weights * point_energy(dens_point, grad_square, kinetic))

    unused, pullback = jax.vjp(energy, start)
    return pullback(jnp.ones((), start.dtype))[0].reshape(count, tile_edge * tile_edge)


def body(
    density,
    three_center,
    metric,
    fetch_owner,
    fetch_slot,
    basis_value,
    basis_gradient,
    pair_slot,
    base_density,
    base_kinetic,
    grid_weight,
):
    devices = lax.axis_size("tile")
    tile_count, width = density.shape
    owner_index = fetch_owner[:, 0]
    every_tile = lax.all_gather(density, "tile", axis=0, tiled=True)
    fetched = every_tile[owner_index * tile_count + fetch_slot]
    aux_blocks, list_length = (three_center.shape[0], three_center.shape[1])
    coul_rows = aux_blocks * list_length
    coul_tiles = fetched[:coul_rows].reshape(aux_blocks, list_length, width)
    source = jnp.einsum(
        "arkp,ark->ap", three_center, coul_tiles, preferred_element_type=jnp.float32
    )
    fit_coef = jnp.einsum("apq,aq->ap", metric, source, precision=lax.Precision.HIGHEST).astype(
        jnp.bfloat16
    )
    coul_part = jnp.einsum(
        "arkp,ap->ark", three_center, fit_coef, preferred_element_type=jnp.float32
    ).reshape(coul_rows, width)
    batches, batch_refs = (pair_slot.shape[0], pair_slot.shape[1])
    xc_tiles = fetched[coul_rows:].reshape(batches, batch_refs, width)
    xc_part = lax.map(
        batch_potential,
        (basis_value, basis_gradient, pair_slot, xc_tiles, base_density, base_kinetic, grid_weight),
    )
    xc_part = xc_part.reshape(batches * batch_refs, width)
    tile_index = owner_index * tile_count + fetch_slot
    coul_full = (
        jnp.zeros((devices * tile_count, width), jnp.float32)
        .at[tile_index[:coul_rows]]
        .add(coul_part)
    )
    xc_full = (
        jnp.zeros((devices * tile_count, width), jnp.float32)
        .at[tile_index[coul_rows:]]
        .add(xc_part)
    )
    coulomb, exchange_corr = (
        lax.psum_scatter(coul_full, "tile", scatter_dimension=0, tiled=True),
        lax.psum_scatter(xc_full, "tile", scatter_dimension=0, tiled=True),
    )
    return (coulomb, exchange_corr)


def solution(mesh):
    in_specs = (
        P(("parts", "tile"), None),
        P(("parts", "tile"), None, None, None),
        P(("parts", "tile"), None, None),
        P(("parts", "tile"), None),
        P(("parts", "tile")),
        P(("parts", "tile"), None, None, None),
        P(("parts", "tile"), None, None, None, None),
        P(("parts", "tile"), None, None),
        P(("parts", "tile"), None),
        P(("parts", "tile"), None),
        P(("parts", "tile"), None),
    )
    out_specs = (P(("parts", "tile"), None), P(("parts", "tile"), None))
    return jax.shard_map(body, mesh=mesh, in_specs=in_specs, out_specs=out_specs, check_vma=False)
```

profile of v0, /device:TPU:0, one launch (start us, length us, event | category | flops | bytes accessed | tf_op | source)
XLA Modules:
  0.0 207.9 jit_solution(909557730095343137)
XLA Ops:
  7.2 0.7 multiply_reduce_fusion.4
  8.0 0.7 compare_select_fusion.2
  8.7 23.7 %all_gather.3 = bf16[256,256]{1,0:T(8,128)(2,1)S(1)} all-gather(bf16[16,256]{1,0:T(8,128)(2,1)} %param.13), channel_id=1, replica_groups=mesh['parts'=2,'tile'=16] {'tile'}, dimensions={0}, use_global_device_ids=true | all-gather | bytes 139264 | tf_op jit(solution)/shard_map/all_gather | solution.py:70
  32.3 2.0 gather_fusion.2
  34.4 52.4 %while.13 = (s32[]{:T(128)}, f32[4,64,256]{2,1,0:T(8,128)}, bf16[4,32,16,128]{3,2,1,0:T(8,128)(2,1)}, bf16[4,32,3,16,128]{4,3,2,1,0:T(8,128)(2,1)}, s32[4,64,2]{...) while((s32[]{:T(128)}, f32[4,64,256]{2,1,0:T(8,128)}, ...), condition=%wide.region_8.9_spmd, body=%wide.region_2.8_spmd.sunk | while | flops 39864320 | bytes 50550596 | solution.py:86
  34.4 0.7 fusion.73
  35.1 1.0 dynamic-slice_bitcast_fusion.4
  36.2 0.9 dynamic-slice_bitcast_fusion.5
  37.2 0.7 gather_fusion.1
  38.4 1.8 convolution_bitcast_fusion.2
  40.1 0.7 gather_fusion
  40.8 1.4 multiply_reduce_fusion.10
  42.2 1.1 slice_bitcast_fusion.5
  43.3 0.6 multiply_reduce_fusion.8
  44.0 0.7 fusion.75
  45.3 0.8 copy-done.3
  46.0 0.5 fusion.76
  46.9 0.6 constant_dynamic-update-slice_fusion.2
  47.5 0.7 fusion.73
  48.2 1.0 dynamic-slice_bitcast_fusion.4
  49.2 0.9 dynamic-slice_bitcast_fusion.5
  50.3 0.7 gather_fusion.1
  51.5 1.8 convolution_bitcast_fusion.2
  53.2 0.7 gather_fusion
  53.9 1.4 multiply_reduce_fusion.10
  55.3 1.1 slice_bitcast_fusion.5
  56.4 0.6 multiply_reduce_fusion.8
  57.1 0.7 fusion.75
  58.4 0.8 copy-done.3
  59.1 0.5 fusion.76
  60.0 0.6 constant_dynamic-update-slice_fusion.2
  60.6 0.7 fusion.73
  61.3 1.0 dynamic-slice_bitcast_fusion.4
  62.3 0.9 dynamic-slice_bitcast_fusion.5
  63.4 0.7 gather_fusion.1
  64.6 1.8 convolution_bitcast_fusion.2
  66.3 0.7 gather_fusion
  67.0 1.4 multiply_reduce_fusion.10
  68.4 1.1 slice_bitcast_fusion.5
  69.5 0.6 multiply_reduce_fusion.8
  70.2 0.7 fusion.75
  71.5 0.8 copy-done.3
  72.2 0.5 fusion.76
  73.1 0.6 constant_dynamic-update-slice_fusion.2
  73.7 0.7 fusion.73
  74.4 1.0 dynamic-slice_bitcast_fusion.4
  75.4 0.9 dynamic-slice_bitcast_fusion.5
  76.5 0.7 gather_fusion.1
  77.6 1.8 convolution_bitcast_fusion.2
  79.4 0.7 gather_fusion
  80.1 1.4 multiply_reduce_fusion.10
  81.5 1.1 slice_bitcast_fusion.5
  82.6 0.6 multiply_reduce_fusion.8
  83.3 0.7 fusion.75
  84.6 0.8 copy-done.3
  85.3 0.5 fusion.76
  86.2 0.6 constant_dynamic-update-slice_fusion.2
  86.9 3.0 %scatter_custom_fusion.1 = f32[256,256]{1,0:T(8,128)} fusion(s32[256]{0:T(256)S(1)} %compare_select_fusion.3, f32[256,256]{1,0:T(8,128)} %bitcast.26, f32[]{:T(128)} %constant.164.clone.1), kind=kCustom, calls=%fused_computation.83 | custom fusion | flops 65536 | bytes 262656 | tf_op jit(solution)/shard_map/scatter-add | solution.py:100
  90.0 3.9 %fusion.37 = f32[3,1,128,1]{2,1,3,0:T(1,128)S(1)} fusion(bf16[3,32,256,128]{3,2,1,0:T(8,128)(2,1)} %param.14, bf16[3,32,256,1]{2,1,0,3:T(8,128)(2,1)S(1)} %bitcast.133), kind=kOutput, calls=%fused_computation.87 | convolution fusion | flops 6291456 | bytes 6342144 | tf_op jit(solution)/shard_map/arkp,ark->ap/dot_general | solution.py:75
  93.9 0.4 fusion.41
  94.6 1.7 fusion.39
  96.4 1.8 scatter_custom_fusion
  98.1 44.5 %reduce-scatter.5.cloned.1.call-done = f32[16,256]{1,0:T(8,128)} async-done(((f32[256,256]{1,0:T(8,128)}), f32[16,256]{1,0:T(8,128)}) %reduce-scatter.5.cloned.1.call-update) | async-done | bytes 16400 | tf_op jit(solution)/shard_map/reduce_scatter | solution.py:104
  142.7 58.4 %reduce-scatter.3.cloned.1.call-done = f32[16,256]{1,0:T(8,128)} async-done(((f32[256,256]{1,0:T(8,128)}), f32[16,256]{1,0:T(8,128)}) %reduce-scatter.3.cloned.1.call-update) | async-done | bytes 16400 | tf_op jit(solution)/shard_map/reduce_scatter | solution.py:103
  (129 shorter events, 6.6 us)
Async XLA Ops:
  7.2 86.8 %copy-start = (f32[3,128,128]{2,1,0:T(8,128)S(1)}, f32[3,128,128]{2,1,0:T(8,128)}, u32[]{:S(2)}) copy-start(f32[3,128,128]{2,1,0:T(8,128)} %param.15) | copy-start | bytes 589828
  7.2 135.5 %reduce-scatter.5.cloned.1.call-start = ((), (), s32[]{:S(2)}) async-start(), calls=%async_computation.3 | async-start | bytes 278528 | tf_op jit(solution)/shard_map/reduce_scatter | solution.py:104
  34.4 3.6 %copy-start.5 = (bf16[4,64,256]{2,1,0:T(8,128)(2,1)}, bf16[4,64,256]{2,1,0:T(8,128)(2,1)S(1)}, u32[]{:S(2)}) copy-start(bf16[4,64,256]{2,1,0:T(8,128)(2,1)S(1)} %get-tuple-element.325) | copy-start | bytes 393220 | tf_op jit(solution)/shard_map/while
  37.9 2.2 %copy-start.2 = (bf16[64,4,16,128]{3,2,1,0:T(8,128)(2,1)}, bf16[64,4,16,128]{3,2,1,0:T(8,128)(2,1)S(1)}, u32[]{:S(2)}) copy-start(bf16[64,4,16,128]{3,2,1,0:T(8,128)(2,1)S(1)} %gather_fusion.1) | copy-start | bytes 3145732 | tf_op jit(solution)/shard_map/while
  40.8 2.5 %copy-start.1 = (f32[64,4,16,128]{3,2,1,0:T(8,128)S(1)}, f32[64,4,16,128]{3,2,1,0:T(8,128)}, u32[]{:S(2)}) copy-start(f32[64,4,16,128]{3,2,1,0:T(8,128)} %convolution_bitcast_fusion.2) | copy-start | bytes 6291460 | tf_op jit(solution)/shard_map/while
  43.3 0.7 copy-start.7
  43.3 0.7 copy-start.8
  44.8 1.2 copy-start.3
  46.0 1.5 copy-start.6
  47.5 3.5 %copy-start.5 = (bf16[4,64,256]{2,1,0:T(8,128)(2,1)}, bf16[4,64,256]{2,1,0:T(8,128)(2,1)S(1)}, u32[]{:S(2)}) copy-start(bf16[4,64,256]{2,1,0:T(8,128)(2,1)S(1)} %get-tuple-element.325) | copy-start | bytes 393220 | tf_op jit(solution)/shard_map/while
  51.0 2.2 %copy-start.2 = (bf16[64,4,16,128]{3,2,1,0:T(8,128)(2,1)}, bf16[64,4,16,128]{3,2,1,0:T(8,128)(2,1)S(1)}, u32[]{:S(2)}) copy-start(bf16[64,4,16,128]{3,2,1,0:T(8,128)(2,1)S(1)} %gather_fusion.1) | copy-start | bytes 3145732 | tf_op jit(solution)/shard_map/while
  53.9 2.5 %copy-start.1 = (f32[64,4,16,128]{3,2,1,0:T(8,128)S(1)}, f32[64,4,16,128]{3,2,1,0:T(8,128)}, u32[]{:S(2)}) copy-start(f32[64,4,16,128]{3,2,1,0:T(8,128)} %convolution_bitcast_fusion.2) | copy-start | bytes 6291460 | tf_op jit(solution)/shard_map/while
  56.4 0.7 copy-start.7
  56.4 0.7 copy-start.8
  57.9 1.2 copy-start.3
  59.1 1.5 copy-start.6
  60.6 3.5 %copy-start.5 = (bf16[4,64,256]{2,1,0:T(8,128)(2,1)}, bf16[4,64,256]{2,1,0:T(8,128)(2,1)S(1)}, u32[]{:S(2)}) copy-start(bf16[4,64,256]{2,1,0:T(8,128)(2,1)S(1)} %get-tuple-element.325) | copy-start | bytes 393220 | tf_op jit(solution)/shard_map/while
  64.1 2.2 %copy-start.2 = (bf16[64,4,16,128]{3,2,1,0:T(8,128)(2,1)}, bf16[64,4,16,128]{3,2,1,0:T(8,128)(2,1)S(1)}, u32[]{:S(2)}) copy-start(bf16[64,4,16,128]{3,2,1,0:T(8,128)(2,1)S(1)} %gather_fusion.1) | copy-start | bytes 3145732 | tf_op jit(solution)/shard_map/while
  67.0 2.5 %copy-start.1 = (f32[64,4,16,128]{3,2,1,0:T(8,128)S(1)}, f32[64,4,16,128]{3,2,1,0:T(8,128)}, u32[]{:S(2)}) copy-start(f32[64,4,16,128]{3,2,1,0:T(8,128)} %convolution_bitcast_fusion.2) | copy-start | bytes 6291460 | tf_op jit(solution)/shard_map/while
  69.5 0.7 copy-start.7
  69.5 0.7 copy-start.8
  71.0 1.2 copy-start.3
  72.2 1.5 copy-start.6
  73.7 3.5 %copy-start.5 = (bf16[4,64,256]{2,1,0:T(8,128)(2,1)}, bf16[4,64,256]{2,1,0:T(8,128)(2,1)S(1)}, u32[]{:S(2)}) copy-start(bf16[4,64,256]{2,1,0:T(8,128)(2,1)S(1)} %get-tuple-element.325) | copy-start | bytes 393220 | tf_op jit(solution)/shard_map/while
  77.2 2.2 %copy-start.2 = (bf16[64,4,16,128]{3,2,1,0:T(8,128)(2,1)}, bf16[64,4,16,128]{3,2,1,0:T(8,128)(2,1)S(1)}, u32[]{:S(2)}) copy-start(bf16[64,4,16,128]{3,2,1,0:T(8,128)(2,1)S(1)} %gather_fusion.1) | copy-start | bytes 3145732 | tf_op jit(solution)/shard_map/while
  80.1 2.5 %copy-start.1 = (f32[64,4,16,128]{3,2,1,0:T(8,128)S(1)}, f32[64,4,16,128]{3,2,1,0:T(8,128)}, u32[]{:S(2)}) copy-start(f32[64,4,16,128]{3,2,1,0:T(8,128)} %convolution_bitcast_fusion.2) | copy-start | bytes 6291460 | tf_op jit(solution)/shard_map/while
  82.6 0.7 copy-start.7
  82.6 0.7 copy-start.8
  84.1 1.2 copy-start.3
  85.3 1.5 copy-start.6
  89.9 111.1 %reduce-scatter.3.cloned.1.call-start = ((), (), s32[]{:S(2)}) async-start(), calls=%async_computation.2 | async-start | bytes 278528 | tf_op jit(solution)/shard_map/reduce_scatter | solution.py:103
  90.0 4.6 %copy-start.4 = (bf16[3,32,256,128]{3,2,1,0:T(8,128)(2,1)S(1)}, bf16[3,32,256,128]{3,2,1,0:T(8,128)(2,1)}, u32[]{:S(2)}) copy-start(bf16[3,32,256,128]{3,2,1,0:T(8,128)(2,1)} %param.14) | copy-start | bytes 18874372
Sparse Core Ops, SparseCore 0:
  90.0 52.5 reduce-scatter.4
  146.7 54.2 reduce-scatter.2
where the time goes:
time: 209 us; the launch traced here: 208 us
  waiting for transfers between devices  103 us (49%)
  local copies, waits for them, and re-layouts  32 us (15%)
  blocking collectives  23.7 us (11%)
  other arithmetic  19.4 us (9%)
  matrix products  15 us (7%)
  between operations  14.1 us (7%)
    reduce_scatter x1, waiting for transfers between devices, body(): lax.psum_scatter(coul_full, 'tile', scatter_dimension=0, tiled=True)  58.4 us
    reduce_scatter x1, waiting for transfers between devices, body(): lax.psum_scatter(xc_full, 'tile', scatter_dimension=0, tiled=True)  44.5 us
    all_gather x1, blocking collectives, body(): every_tile = lax.all_gather(density, 'tile', axis=0, tiled=True)  23.7 us
    dot_general x8, matrix products, energy(): mixed_terms = jnp.einsum('rmn,rcng->rcmg', tile_values, right_basis)  8.98 us
    squeeze x8, local copies, waits for them, and re-layouts, body(): lax.map(batch_potential, (basis_value, basis_gradient, pair_slot, xc_tile...  6.85 us
    reduce_sum x4, other arithmetic, energy(): point_rho = jnp.sum(left_basis[:, 0] * mixed_terms[:, 0], axis=(0, 1))  5.41 us
    mul x4, local copies, waits for them, and re-layouts, energy(): left_basis[:, 1:] * mixed_terms[:, :1]  4.33 us
  transfers between devices with their start and end apart: 2, of which 2 were waited for; matrix products, arithmetic and copies ran while one was open for 4% of the time, Pallas kernels for 0%

commit v1 on v0

v1 whole, which is shorter than its diff:
```python
import functools

import jax
import jax.numpy as jnp
from jax import lax
from jax.experimental import pallas as pl
from jax.experimental.pallas import tpu as pltpu
from jax.sharding import PartitionSpec as P

CX_COEF = 0.7385587663820224
CS_COEF = 0.026121172985233605
CTF_COEF = 2.871234000188191
KAPPA_VALUE = 0.804
MU_COEF = 0.12345679012345678
H_ZERO = 1.174

F32 = jnp.float32
BF16 = jnp.bfloat16
LANES = 128


def dot(left, right):
    return lax.dot_general(left, right, (((1,), (0,)), ((), ())), preferred_element_type=F32)


def dot_nt(left, right, precision=None):
    return lax.dot_general(
        left, right, (((1,), (1,)), ((), ())), precision=precision, preferred_element_type=F32
    )


def dot_tn(left, right):
    return lax.dot_general(left, right, (((0,), (0,)), ((), ())), preferred_element_type=F32)


def iota(shape, dim):
    return lax.broadcasted_iota(jnp.int32, shape, dim)


def one_hot(condition):
    return jnp.where(condition, 1.0, 0.0).astype(BF16)


def smooth_floor(amount):
    return 0.5 * (amount + jnp.sqrt(amount * amount + 1.0))


def point_energy(grid_rho, grad_x, grad_y, grad_z, grid_tau, base_rho, base_tau, weights):
    rho = smooth_floor(base_rho + grid_rho)
    tau = smooth_floor(base_tau + grid_tau)
    sigma = grad_x * grad_x + grad_y * grad_y + grad_z * grad_z
    root = jnp.exp(jnp.log(rho) * (1.0 / 3.0))
    five = rho * root * root
    s_square = CS_COEF * sigma / (rho * five)
    h_one = 1.0 + KAPPA_VALUE - KAPPA_VALUE / (1.0 + MU_COEF * s_square / KAPPA_VALUE)
    iso_alpha = (tau - sigma / (8.0 * rho)) / (CTF_COEF * five)
    factor = h_one + (H_ZERO - h_one) / (1.0 + iso_alpha * iso_alpha)
    return weights * (-CX_COEF * (rho * root) * factor)


def kernel(
    sizes,
    density_hbm,
    metric_hbm,
    owner_hbm,
    slot_hbm,
    pair_hbm,
    base_rho_hbm,
    base_tau_hbm,
    weight_hbm,
    three_hbm,
    value_hbm,
    slope_hbm,
    coul_out,
    xc_out,
    owner_ref,
    slot_ref,
    pair_ref,
    base_rho_ref,
    base_tau_ref,
    weight_ref,
    metric_ref,
    table,
    three,
    basis,
    left,
    spread,
    fetched,
    dense,
    dense_low,
    masks,
    takes,
    gathered,
    coul_rows_s,
    xc_rows_s,
    points,
    slopes,
    coul_send,
    xc_send,
    coul_recv,
    xc_recv,
    local_sem,
    gather_send_sem,
    gather_recv_sem,
    coul_send_sem,
    coul_recv_sem,
    xc_send_sem,
    xc_recv_sem,
):
    devices, tile_count, width, aux, listed, batches, refs, blocks, edge, grid = sizes
    coul_rows = aux * listed
    basis_rows = blocks * edge
    edge_bits = edge.bit_length() - 1
    block_bits = blocks.bit_length() - 1
    lane_bits = grid.bit_length() - 1
    total_tiles = devices * tile_count
    me = lax.axis_index("tile")

    own_rows = pl.ds(pl.multiple_of(me * tile_count, tile_count), tile_count)
    moves = [
        (density_hbm, table.at[own_rows]),
        (owner_hbm, owner_ref),
        (slot_hbm, slot_ref),
        (pair_hbm, pair_ref),
        (value_hbm, basis.at[:, :, :, 0:grid]),
    ]
    for c in range(3):
        moves.append(
            (slope_hbm.at[:, :, c], basis.at[:, :, :, (c + 1) * grid : (c + 2) * grid])
        )
    moves += [
        (three_hbm, three),
        (metric_hbm, metric_ref),
        (base_rho_hbm, base_rho_ref),
        (base_tau_hbm, base_tau_ref),
        (weight_hbm, weight_ref),
    ]
    copies = [
        pltpu.make_async_copy(source, target, local_sem.at[k])
        for k, (source, target) in enumerate(moves)
    ]

    barrier = pltpu.get_barrier_semaphore()

    def greet(shift, carry):
        peer = lax.rem(me + shift, devices)
        pl.semaphore_signal(
            barrier, inc=1, device_id={"tile": peer}, device_id_type=pl.DeviceIdType.MESH
        )
        return carry

    lax.fori_loop(1, devices, greet, 0)
    for copy in copies:
        copy.start()

    def send(source, target, send_sem, recv_sem, shift):
        return pltpu.make_async_remote_copy(
            src_ref=source,
            dst_ref=target,
            send_sem=send_sem.at[shift],
            recv_sem=recv_sem.at[shift],
            device_id={"tile": lax.rem(me + shift, devices)},
            device_id_type=pl.DeviceIdType.MESH,
        )

    def tile_rows(ref, owner):
        return ref.at[pl.ds(pl.multiple_of(owner * tile_count, tile_count), tile_count)]

    copies[0].wait()
    pl.semaphore_wait(barrier, devices - 1)

    def gather_start(shift, carry):
        send(tile_rows(table, me), tile_rows(table, me), gather_send_sem, gather_recv_sem, shift).start()
        return carry

    lax.fori_loop(1, devices, gather_start, 0)

    spread_width = edge * LANES
    row = iota((width, spread_width), 0)
    lane = iota((width, spread_width), 1)
    spread[...] = one_hot(
        (jnp.right_shift(row, edge_bits) == jnp.right_shift(lane, 7))
        & ((row & (edge - 1)) == (lane & (edge - 1)))
    )
    row = iota((basis_rows, basis_rows), 0)
    lane = iota((basis_rows, basis_rows), 1)
    order = one_hot(lane == ((row & (blocks - 1)) << edge_bits) + jnp.right_shift(row, block_bits))
    for copy in copies[1:4]:
        copy.wait()
    drop = one_hot(
        owner_ref[...] * tile_count + slot_ref[...]
        == iota((total_tiles, coul_rows + batches * refs), 0)
    )
    same = one_hot(
        iota((blocks, basis_rows), 0) == jnp.right_shift(iota((blocks, basis_rows), 1), edge_bits)
    )
    unit = one_hot(iota((blocks, blocks), 0) == iota((blocks, blocks), 1))
    for b in range(batches):
        block_row = iota((blocks, refs), 0)
        masks[b] = dot_tn(one_hot(pair_ref[b, 1:2, :] == block_row), same).astype(BF16)
        takes[b] = dot_tn(one_hot(pair_ref[b, 0:1, :] == block_row), unit).astype(BF16)
    for copy in copies[4:8]:
        copy.wait()

    def reorder(b, carry):
        left[b] = dot(order, basis[b].reshape(basis_rows, 4 * grid)).astype(BF16)
        return carry

    lax.fori_loop(0, batches, reorder, 0)

    def gather_wait(shift, carry):
        owner = lax.rem(me - shift + devices, devices)
        copy = send(tile_rows(table, me), tile_rows(table, owner), gather_send_sem, gather_recv_sem, shift)
        copy.wait_recv()
        copy.wait_send()
        return carry

    lax.fori_loop(1, devices, gather_wait, 0)

    picked = dot_tn(drop, table[...])
    coul_tiles = picked[:coul_rows]
    fetched[...] = dot(picked[coul_rows:].astype(BF16), spread[...]).astype(BF16)

    copies[8].wait()
    copies[9].wait()
    for a in range(aux):
        source = jnp.zeros((1, grid), F32)
        for r in range(listed):
            k = a * listed + r
            source = source + dot(coul_tiles[k : k + 1].astype(BF16), three[a, r])
        coef = dot_nt(source, metric_ref[a], lax.Precision.HIGHEST).astype(BF16)
        for r in range(listed):
            k = a * listed + r
            coul_rows_s[k : k + 1, :] = dot_nt(coef, three[a, r])
    part = coul_rows_s[...]
    high = part.astype(BF16)
    low = (part - high.astype(F32)).astype(BF16)
    drop_coul = drop[:, :coul_rows]
    coul_send[...] = (dot(drop_coul, high) + dot(drop_coul, low)).astype(BF16)

    def push(source, recv, send_sem, recv_sem):
        def start(shift, carry):
            peer = lax.rem(me + shift, devices)
            send(tile_rows(source, peer), recv.at[shift], send_sem, recv_sem, shift).start()
            return carry

        lax.fori_loop(1, devices, start, 0)

    def total(source, recv, send_sem, recv_sem):
        own = source[pl.ds(pl.multiple_of(me * tile_count, tile_count), tile_count), :]

        def add(shift, so_far):
            peer = lax.rem(me + shift, devices)
            copy = send(tile_rows(source, peer), recv.at[shift], send_sem, recv_sem, shift)
            copy.wait_recv()
            copy.wait_send()
            return so_far + recv[shift].astype(F32)

        return lax.fori_loop(1, devices, add, own.astype(F32))

    push(coul_send, coul_recv, coul_send_sem, coul_recv_sem)

    chunk = min(basis_rows, 128)

    def batch_rows(b):
        return pl.ds(pl.multiple_of(b * refs, refs), refs)

    copies_across = basis_rows // LANES

    def forward(b, carry):
        mask, rows = masks[b], batch_rows(b)
        place = one_hot(pair_ref[b, 0:1, :] == iota((blocks, refs), 0))
        for m in range(edge):
            part = fetched[rows, m * LANES : (m + 1) * LANES]
            wide = jnp.concatenate([part] * copies_across, axis=1) * mask
            full = dot(place, wide)
            high = full.astype(BF16)
            dense[m * blocks : (m + 1) * blocks, :] = high
            dense_low[m * blocks : (m + 1) * blocks, :] = (full - high.astype(F32)).astype(BF16)
        right = basis[b].reshape(basis_rows, 4 * grid)
        sums = [jnp.zeros((8, grid), F32) for unused in range(5)]
        for start in range(0, basis_rows, chunk):
            mixed = dot(dense[start : start + chunk, :], right)
            mixed = mixed + dot(dense_low[start : start + chunk, :], right)
            lefts = left[b, start : start + chunk, :].astype(F32)

            def part(array, c):
                return array[:, c * grid : (c + 1) * grid]

            l0, m0 = part(lefts, 0), part(mixed, 0)
            terms = [l0 * m0]
            tau = None
            for c in range(1, 4):
                lc, mc = part(lefts, c), part(mixed, c)
                terms.append(lc * m0 + l0 * mc)
                tau = lc * mc if tau is None else tau + lc * mc
            terms.append(tau)
            for q in range(5):
                sums[q] = sums[q] + jnp.sum(terms[q].reshape(chunk // 8, 8, grid), axis=0)
        for q in range(5):
            points[q, pl.ds(b, 1), :] = jnp.sum(sums[q], axis=0, keepdims=True)
        return carry

    lax.fori_loop(0, batches, forward, 0)

    for copy in copies[10:]:
        copy.wait()
    base_rho, base_tau, weights = base_rho_ref[...], base_tau_ref[...], weight_ref[...]

    def energy(grid_rho, grad_x, grad_y, grad_z, grid_tau):
        return point_energy(
            grid_rho, grad_x, grad_y, grad_z, grid_tau, base_rho, base_tau, weights
        )

    values = [points[q] for q in range(5)]
    values[4] = 0.5 * values[4]
    unused, pullback = jax.vjp(energy, *values)
    found = pullback(jnp.ones_like(weights))
    for q in range(5):
        slopes[q] = 0.5 * found[q] if q == 4 else found[q]

    def backward(b, carry):
        mask, take, rows = masks[b].astype(F32), takes[b], batch_rows(b)
        by = [slopes[q, pl.ds(b, 1), :] for q in range(5)]
        right = basis[b].reshape(basis_rows, 4 * grid).astype(F32)
        part = [right[:, c * grid : (c + 1) * grid] for c in range(4)]
        bent = [by[0] * part[0] + by[1] * part[1] + by[2] * part[2] + by[3] * part[3]]
        for c in range(1, 4):
            bent.append(by[c] * part[0] + by[4] * part[c])
        bent = jnp.concatenate([each.astype(BF16) for each in bent], axis=1)
        per = max(1, chunk // blocks)
        for m in range(0, edge, per):
            outer = dot_nt(left[b, m * blocks : (m + per) * blocks, :], bent).astype(BF16)
            for s in range(per):
                own = dot(take, outer[s * blocks : (s + 1) * blocks]) * mask
                folded = own[:, :LANES]
                for q in range(1, copies_across):
                    folded = folded + own[:, q * LANES : (q + 1) * LANES]
                gathered[:, (m + s) * LANES : (m + s + 1) * LANES] = folded.astype(BF16)
        xc_rows_s[rows, :] = dot_nt(gathered[...], spread[...]).astype(BF16)
        return carry

    lax.fori_loop(0, batches, backward, 0)
    xc_send[...] = dot(drop[:, coul_rows:], xc_rows_s[...]).astype(BF16)
    push(xc_send, xc_recv, xc_send_sem, xc_recv_sem)
    coul_out[...] = total(coul_send, coul_recv, coul_send_sem, coul_recv_sem)
    xc_out[...] = total(xc_send, xc_recv, xc_send_sem, xc_recv_sem)


def body(
    density,
    three_center,
    metric,
    fetch_owner,
    fetch_slot,
    basis_value,
    basis_gradient,
    pair_slot,
    base_density,
    base_kinetic,
    grid_weight,
):
    devices = lax.axis_size("tile")
    tile_count, width = density.shape
    aux, listed = three_center.shape[:2]
    batches, refs = pair_slot.shape[:2]
    blocks, edge, grid = basis_value.shape[1:]
    coul_rows = aux * listed
    total_refs = coul_rows + batches * refs
    sizes = (devices, tile_count, width, aux, listed, batches, refs, blocks, edge, grid)
    vmem = pl.BlockSpec(memory_space=pltpu.VMEM)
    far = pl.BlockSpec(memory_space=pl.ANY)
    total_tiles = devices * tile_count
    basis_rows = blocks * edge
    out = jax.ShapeDtypeStruct((tile_count, width), F32)
    semaphores = pltpu.SemaphoreType.DMA((devices,))
    return pl.pallas_call(
        functools.partial(kernel, sizes),
        out_shape=(out, out),
        in_specs=[far] * 11,
        out_specs=(vmem, vmem),
        scratch_shapes=[
            pltpu.VMEM((1, total_refs), jnp.int32),
            pltpu.VMEM((1, total_refs), jnp.int32),
            pltpu.VMEM((batches, 2, refs), jnp.int32),
            pltpu.VMEM((batches, grid), F32),
            pltpu.VMEM((batches, grid), F32),
            pltpu.VMEM((batches, grid), F32),
            pltpu.VMEM(metric.shape, F32),
            pltpu.VMEM((total_tiles, width), BF16),
            pltpu.VMEM(three_center.shape, BF16),
            pltpu.VMEM((batches, blocks, edge, 4 * grid), BF16),
            pltpu.VMEM((batches, basis_rows, 4 * grid), BF16),
            pltpu.VMEM((width, edge * LANES), BF16),
            pltpu.VMEM((batches * refs, edge * LANES), BF16),
            pltpu.VMEM((basis_rows, basis_rows), BF16),
            pltpu.VMEM((basis_rows, basis_rows), BF16),
            pltpu.VMEM((batches, refs, basis_rows), BF16),
            pltpu.VMEM((batches, refs, blocks), BF16),
            pltpu.VMEM((refs, edge * LANES), BF16),
            pltpu.VMEM((coul_rows, width), F32),
            pltpu.VMEM((batches * refs, width), BF16),
            pltpu.VMEM((5, batches, grid), F32),
            pltpu.VMEM((5, batches, grid), F32),
            pltpu.VMEM((total_tiles, width), BF16),
            pltpu.VMEM((total_tiles, width), BF16),
            pltpu.VMEM((devices, tile_count, width), BF16),
            pltpu.VMEM((devices, tile_count, width), BF16),
            pltpu.SemaphoreType.DMA((13,)),
            semaphores,
            semaphores,
            semaphores,
            semaphores,
            semaphores,
            semaphores,
        ],
        compiler_params=pltpu.CompilerParams(
            collective_id=0, has_side_effects=True, vmem_limit_bytes=60 * 1024 * 1024
        ),
        name="fock_build",
    )(
        density,
        metric,
        fetch_owner.reshape(1, total_refs),
        fetch_slot.reshape(1, total_refs),
        jnp.swapaxes(pair_slot, 1, 2),
        base_density,
        base_kinetic,
        grid_weight,
        three_center,
        basis_value,
        basis_gradient,
    )


def solution(mesh):
    in_specs = (
        P(("parts", "tile"), None),
        P(("parts", "tile"), None, None, None),
        P(("parts", "tile"), None, None),
        P(("parts", "tile"), None),
        P(("parts", "tile")),
        P(("parts", "tile"), None, None, None),
        P(("parts", "tile"), None, None, None, None),
        P(("parts", "tile"), None, None),
        P(("parts", "tile"), None),
        P(("parts", "tile"), None),
        P(("parts", "tile"), None),
    )
    out_specs = (P(("parts", "tile"), None), P(("parts", "tile"), None))
    return jax.shard_map(body, mesh=mesh, in_specs=in_specs, out_specs=out_specs, check_vma=False)
```

time: 209 us -> 40.2 us (0.19)
  waiting for transfers between devices: 103 us -> 0 us
  Pallas kernels: 0 us -> 35.2 us
  local copies, waits for them, and re-layouts: 32 us -> 3.89 us
  blocking collectives: 23.7 us -> 0 us
  other arithmetic: 19.4 us -> 0 us
  matrix products: 15 us -> 0 us
  between operations: 14.1 us -> 0.64 us
    reduce_scatter x2 -> x0, waiting for transfers between devices: 103 us -> none  [the longest x1 58.4 us: body(): lax.psum_scatter(coul_full, 'tile', scatter_dimension=0, tiled=True)]
    pallas_call x0 -> x1, Pallas kernels: none -> 35.2 us  [body(): pl.pallas_call(functools.partial(kernel, sizes), out_shape=(out, out), in...]
    all_gather x1 -> x0, blocking collectives: 23.7 us -> none  [body(): every_tile = lax.all_gather(density, 'tile', axis=0, tiled=True)]
    dot_general x11 -> x0, matrix products: 15 us -> none  [the longest x8 8.98 us: energy(): mixed_terms = jnp.einsum('rmn,rcng->rcmg', tile_values, right_basis)]
    gather x9 -> x0, local copies, waits for them, and re-layouts: 7.76 us -> none  [the longest x4 3 us: batch_potential(): right_basis = basis[slot_pairs[:, 1]]]
    reduce_sum x12 -> x0, other arithmetic: 7.75 us -> none  [the longest x4 5.41 us: energy(): point_rho = jnp.sum(left_basis[:, 0] * mixed_terms[:, 0], axis=(0, 1))]
    squeeze x8 -> x0, local copies, waits for them, and re-layouts: 6.85 us -> none  [body(): lax.map(batch_potential, (basis_value, basis_gradient, pair_slot, xc_tile...]
    mul x13 -> x0, other arithmetic: 5.23 us -> none  [the longest x4 2.95 us: energy(): 0.5 * jnp.sum(left_basis[:, 1:] * mixed_terms[:, 1:], axis=(0, 1, 2))]
  transfers between devices with their start and end apart: 2 -> 0, of which waited for: 2 -> 0; matrix products, arithmetic and copies ran while one was open for 4% -> 0% of each run, Pallas kernels for 0% -> 0%
where the time goes in v1:
time: 40.2 us; the launch traced here: 39.8 us
  Pallas kernels  35.2 us (88%)
  local copies, waits for them, and re-layouts  3.89 us (10%)
  between operations  0.64 us (2%)
    pallas_call x1, Pallas kernels, body(): pl.pallas_call(functools.partial(kernel, sizes), out_shape=(out, out), in...  35.2 us
    unnamed x2, local copies, waits for them, and re-layouts  2.65 us
    reshape x1, local copies, waits for them, and re-layouts, body(): fetch_slot.reshape(1, total_refs)  1.25 us

profile of v1, /device:TPU:0, one launch (start us, length us, event | category | flops | bytes accessed | tf_op | source)
XLA Modules:
  0.0 39.8 jit_solution(12288571697792739711)
XLA Ops:
  0.6 1.2 %reshape.11.slot_hbm = s32[1,352]{1,0:T(1,128)} reshape(s32[352]{0:T(512)} %param.15) | data formatting | bytes 2816 | tf_op jit(solution)/shard_map/reshape | solution.py:425
  1.9 35.2 %fock_build.1 = (f32[16,256]{1,0:T(8,128)}, f32[16,256]{1,0:T(8,128)}) custom-call(bf16[16,256]{1,0:T(8,128)(2,1)} %density_hbm.1, f32[3,128,128]{2,1,0:T(8,128)} %metric_hbm.1, s32[1,352]{1,0:T(1,128)} %bitcast.3, s32[1,352]{1,0:T(1,128)} %reshape.11.slot_hbm, s32[4,2,64]{2,1,0:T(2,128)} %bitcast.2, f32[4,128]{1,0:T(4,128)} %base_rho_hbm.1, ...), custom_call_target="tpu_custom_call" | custom-call | tf_op jit(solution)/shard_map/fock_build/pallas_call | solution.py:377
  37.1 1.3 %copy.15 = f32[16,256]{1,0:T(8,128)} copy(f32[16,256]{1,0:T(8,128)} %get-tuple-element.4) | data formatting | bytes 32768
  38.4 1.3 %copy.16 = f32[16,256]{1,0:T(8,128)} copy(f32[16,256]{1,0:T(8,128)} %get-tuple-element.5) | data formatting | bytes 32768

commit v2 on v1

--- a/solution.py
+++ b/solution.py
@@ -71,8 +71,7 @@
     three_hbm,
     value_hbm,
     slope_hbm,
-    coul_out,
-    xc_out,
+    both_out,
     owner_ref,
     slot_ref,
     pair_ref,
@@ -85,6 +84,10 @@
     basis,
     left,
     spread,
+    gather_up,
+    pick,
+    mixed_s,
+    outer_s,
     fetched,
     dense,
     dense_low,
@@ -92,7 +95,6 @@
     takes,
     gathered,
     coul_rows_s,
-    xc_rows_s,
     points,
     slopes,
     coul_send,
@@ -109,6 +111,7 @@
 ):
     devices, tile_count, width, aux, listed, batches, refs, blocks, edge, grid = sizes
     coul_rows = aux * listed
+    total_refs = coul_rows + batches * refs
     basis_rows = blocks * edge
     edge_bits = edge.bit_length() - 1
     block_bits = blocks.bit_length() - 1
@@ -166,29 +169,26 @@
     def tile_rows(ref, owner):
         return ref.at[pl.ds(pl.multiple_of(owner * tile_count, tile_count), tile_count)]
 
-    copies[0].wait()
-    pl.semaphore_wait(barrier, devices - 1)
-
-    def gather_start(shift, carry):
-        send(tile_rows(table, me), tile_rows(table, me), gather_send_sem, gather_recv_sem, shift).start()
-        return carry
-
-    lax.fori_loop(1, devices, gather_start, 0)
-
-    spread_width = edge * LANES
-    row = iota((width, spread_width), 0)
-    lane = iota((width, spread_width), 1)
-    spread[...] = one_hot(
-        (jnp.right_shift(row, edge_bits) == jnp.right_shift(lane, 7))
-        & ((row & (edge - 1)) == (lane & (edge - 1)))
-    )
-    row = iota((basis_rows, basis_rows), 0)
-    lane = iota((basis_rows, basis_rows), 1)
-    order = one_hot(lane == ((row & (blocks - 1)) << edge_bits) + jnp.right_shift(row, block_bits))
+    spread[...] = jnp.zeros_like(spread)
+    repeat = one_hot(iota((edge, LANES), 0) == (iota((edge, LANES), 1) & (edge - 1)))
+    step = jnp.where(
+        (iota((LANES, width), 0) & (edge - 1)) == (iota((LANES, width), 1) & (edge - 1)), 1.0, 0.0
+    )
+    which = jnp.right_shift(iota((1, width), 1), edge_bits)
+    for m in range(edge):
+        spread[m * edge : (m + 1) * edge, m * LANES : (m + 1) * LANES] = repeat
+        gather_up[m * LANES : (m + 1) * LANES, :] = (
+            step * jnp.where(which == m, 1.0, 0.0)
+        ).astype(BF16)
+    lane = iota((1, basis_rows), 1)
+    order = one_hot(
+        iota((basis_rows, basis_rows), 0)
+        == ((lane & (edge - 1)) << block_bits) + jnp.right_shift(lane, edge_bits)
+    )
     for copy in copies[1:4]:
         copy.wait()
     drop = one_hot(
-        owner_ref[...] * tile_count + slot_ref[...]
+        owner_ref[...] * tile_count + slot_ref[...].reshape(1, total_refs)
         == iota((total_tiles, coul_rows + batches * refs), 0)
     )
     same = one_hot(
@@ -199,6 +199,16 @@
         block_row = iota((blocks, refs), 0)
         masks[b] = dot_tn(one_hot(pair_ref[b, 1:2, :] == block_row), same).astype(BF16)
         takes[b] = dot_tn(one_hot(pair_ref[b, 0:1, :] == block_row), unit).astype(BF16)
+    pick[...] = jnp.transpose(drop.astype(F32)).astype(BF16)
+    copies[0].wait()
+    pl.semaphore_wait(barrier, devices - 1)
+
+    def gather_start(shift, carry):
+        send(tile_rows(table, me), tile_rows(table, me), gather_send_sem, gather_recv_sem, shift).start()
+        return carry
+
+    lax.fori_loop(1, devices, gather_start, 0)
+
     for copy in copies[4:8]:
         copy.wait()
 
@@ -206,7 +216,7 @@
         left[b] = dot(order, basis[b].reshape(basis_rows, 4 * grid)).astype(BF16)
         return carry
 
-    lax.fori_loop(0, batches, reorder, 0)
+    lax.fori_loop(0, batches, reorder, 0, unroll=True)
 
     def gather_wait(shift, carry):
         owner = lax.rem(me - shift + devices, devices)
@@ -217,21 +227,28 @@
 
     lax.fori_loop(1, devices, gather_wait, 0)
 
-    picked = dot_tn(drop, table[...])
+    picked = dot(pick[...], table[...])
     coul_tiles = picked[:coul_rows]
     fetched[...] = dot(picked[coul_rows:].astype(BF16), spread[...]).astype(BF16)
 
     copies[8].wait()
     copies[9].wait()
     for a in range(aux):
-        source = jnp.zeros((1, grid), F32)
-        for r in range(listed):
+        source = jnp.zeros((2, 2 * grid), F32)
+        for r in range(0, listed, 2):
             k = a * listed + r
-            source = source + dot(coul_tiles[k : k + 1].astype(BF16), three[a, r])
-        coef = dot_nt(source, metric_ref[a], lax.Precision.HIGHEST).astype(BF16)
-        for r in range(listed):
+            pair = jnp.concatenate([three[a, r], three[a, r + 1]], axis=1)
+            source = source + dot(coul_tiles[k : k + 2].astype(BF16), pair)
+        source = source[0:1, :grid] + source[1:2, grid:]
+        coef = dot_nt(source, metric_ref[a], lax.Precision.HIGHEST)
+        none = jnp.zeros_like(coef)
+        coef = jnp.concatenate(
+            [jnp.concatenate([coef, none], axis=1), jnp.concatenate([none, coef], axis=1)], axis=0
+        ).astype(BF16)
+        for r in range(0, listed, 2):
             k = a * listed + r
-            coul_rows_s[k : k + 1, :] = dot_nt(coef, three[a, r])
+            pair = jnp.concatenate([three[a, r], three[a, r + 1]], axis=1)
+            coul_rows_s[k : k + 2, :] = dot_nt(coef, pair)
     part = coul_rows_s[...]
     high = part.astype(BF16)
     low = (part - high.astype(F32)).astype(BF16)
@@ -278,10 +295,10 @@
             dense[m * blocks : (m + 1) * blocks, :] = high
             dense_low[m * blocks : (m + 1) * blocks, :] = (full - high.astype(F32)).astype(BF16)
         right = basis[b].reshape(basis_rows, 4 * grid)
+        mixed_s[...] = dot(dense[...], right) + dot(dense_low[...], right)
         sums = [jnp.zeros((8, grid), F32) for unused in range(5)]
         for start in range(0, basis_rows, chunk):
-            mixed = dot(dense[start : start + chunk, :], right)
-            mixed = mixed + dot(dense_low[start : start + chunk, :], right)
+            mixed = mixed_s[start : start + chunk, :]
             lefts = left[b, start : start + chunk, :].astype(F32)
 
             def part(array, c):
@@ -301,7 +318,7 @@
             points[q, pl.ds(b, 1), :] = jnp.sum(sums[q], axis=0, keepdims=True)
         return carry
 
-    lax.fori_loop(0, batches, forward, 0)
+    lax.fori_loop(0, batches, forward, 0, unroll=True)
 
     for copy in copies[10:]:
         copy.wait()
@@ -328,23 +345,32 @@
         for c in range(1, 4):
             bent.append(by[c] * part[0] + by[4] * part[c])
         bent = jnp.concatenate([each.astype(BF16) for each in bent], axis=1)
-        per = max(1, chunk // blocks)
-        for m in range(0, edge, per):
-            outer = dot_nt(left[b, m * blocks : (m + per) * blocks, :], bent).astype(BF16)
-            for s in range(per):
-                own = dot(take, outer[s * blocks : (s + 1) * blocks]) * mask
-                folded = own[:, :LANES]
-                for q in range(1, copies_across):
-                    folded = folded + own[:, q * LANES : (q + 1) * LANES]
-                gathered[:, (m + s) * LANES : (m + s + 1) * LANES] = folded.astype(BF16)
-        xc_rows_s[rows, :] = dot_nt(gathered[...], spread[...]).astype(BF16)
-        return carry
-
-    lax.fori_loop(0, batches, backward, 0)
-    xc_send[...] = dot(drop[:, coul_rows:], xc_rows_s[...]).astype(BF16)
+        outer_s[...] = dot_nt(left[b], bent).astype(BF16)
+        for m in range(edge):
+            own = dot(take, outer_s[m * blocks : (m + 1) * blocks, :]) * mask
+            folded = own[:, :LANES]
+            for q in range(1, copies_across):
+                folded = folded + own[:, q * LANES : (q + 1) * LANES]
+            gathered[rows, m * LANES : (m + 1) * LANES] = folded.astype(BF16)
+        return carry
+
+    lax.fori_loop(0, batches, backward, 0, unroll=True)
+    xc_rows = dot(gathered[...], gather_up[...]).astype(BF16)
+    xc_send[...] = dot(drop[:, coul_rows:], xc_rows).astype(BF16)
     push(xc_send, xc_recv, xc_send_sem, xc_recv_sem)
-    coul_out[...] = total(coul_send, coul_recv, coul_send_sem, coul_recv_sem)
-    xc_out[...] = total(xc_send, xc_recv, xc_send_sem, xc_recv_sem)
+    both_out[0] = total(coul_send, coul_recv, coul_send_sem, coul_recv_sem)
+    both_out[1] = total(xc_send, xc_recv, xc_send_sem, xc_recv_sem)
+
+
+def part_outputs(both_ref, coul_ref, xc_ref, sem):
+    copies = [
+        pltpu.make_async_copy(both_ref.at[0], coul_ref, sem.at[0]),
+        pltpu.make_async_copy(both_ref.at[1], xc_ref, sem.at[1]),
+    ]
+    for copy in copies:
+        copy.start()
+    for copy in copies:
+        copy.wait()
 
 
 def body(
@@ -374,14 +400,14 @@
     basis_rows = blocks * edge
     out = jax.ShapeDtypeStruct((tile_count, width), F32)
     semaphores = pltpu.SemaphoreType.DMA((devices,))
-    return pl.pallas_call(
+    both = pl.pallas_call(
         functools.partial(kernel, sizes),
-        out_shape=(out, out),
+        out_shape=jax.ShapeDtypeStruct((2, tile_count, width), F32),
         in_specs=[far] * 11,
-        out_specs=(vmem, vmem),
+        out_specs=vmem,
         scratch_shapes=[
             pltpu.VMEM((1, total_refs), jnp.int32),
-            pltpu.VMEM((1, total_refs), jnp.int32),
+            pltpu.VMEM((total_refs,), jnp.int32),
             pltpu.VMEM((batches, 2, refs), jnp.int32),
             pltpu.VMEM((batches, grid), F32),
             pltpu.VMEM((batches, grid), F32),
@@ -392,14 +418,17 @@
             pltpu.VMEM((batches, blocks, edge, 4 * grid), BF16),
             pltpu.VMEM((batches, basis_rows, 4 * grid), BF16),
             pltpu.VMEM((width, edge * LANES), BF16),
+            pltpu.VMEM((edge * LANES, width), BF16),
+            pltpu.VMEM((total_refs, total_tiles), BF16),
+            pltpu.VMEM((basis_rows, 4 * grid), F32),
+            pltpu.VMEM((basis_rows, basis_rows), BF16),
             pltpu.VMEM((batches * refs, edge * LANES), BF16),
             pltpu.VMEM((basis_rows, basis_rows), BF16),
             pltpu.VMEM((basis_rows, basis_rows), BF16),
             pltpu.VMEM((batches, refs, basis_rows), BF16),
             pltpu.VMEM((batches, refs, blocks), BF16),
-            pltpu.VMEM((refs, edge * LANES), BF16),
+            pltpu.VMEM((batches * refs, edge * LANES), BF16),
             pltpu.VMEM((coul_rows, width), F32),
-            pltpu.VMEM((batches * refs, width), BF16),
             pltpu.VMEM((5, batches, grid), F32),
             pltpu.VMEM((5, batches, grid), F32),
             pltpu.VMEM((total_tiles, width), BF16),
@@ -422,7 +451,7 @@
         density,
         metric,
         fetch_owner.reshape(1, total_refs),
-        fetch_slot.reshape(1, total_refs),
+        fetch_slot,
         jnp.swapaxes(pair_slot, 1, 2),
         base_density,
         base_kinetic,
@@ -431,6 +460,14 @@
         basis_value,
         basis_gradient,
     )
+    return pl.pallas_call(
+        part_outputs,
+        out_shape=(out, out),
+        in_specs=[far],
+        out_specs=(far, far),
+        scratch_shapes=[pltpu.SemaphoreType.DMA((2,))],
+        name="outputs",
+    )(both)
 
 
 def solution(mesh):

time: 40.2 us -> 32.5 us (0.81)
  local copies, waits for them, and re-layouts: 3.89 us -> 0 us
  Pallas kernels: 35.2 us -> 31.7 us
    pallas_call x1 -> x2, Pallas kernels: 35.2 us -> 31.7 us  [the longest x1 29.6 us: body(): pl.pallas_call(functools.partial(kernel, sizes), out_shape=jax.ShapeDtype...]
    unnamed x2 -> x0, local copies, waits for them, and re-layouts: 2.65 us -> none
    reshape x1 -> x0, local copies, waits for them, and re-layouts: 1.25 us -> none  [body(): fetch_slot.reshape(1, total_refs)]
where the time goes in v2:
time: 32.5 us; the launch traced here: 32.4 us
  Pallas kernels  31.7 us (98%)
  between operations  0.64 us (2%)
    pallas_call x1, Pallas kernels, body(): pl.pallas_call(functools.partial(kernel, sizes), out_shape=jax.ShapeDtype...  29.6 us
    pallas_call x1, Pallas kernels, body(): pl.pallas_call(part_outputs, out_shape=(out, out), in_specs=[far], out_sp...  2.11 us

profile of v2, /device:TPU:0, one launch (start us, length us, event | category | flops | bytes accessed | tf_op | source)
XLA Modules:
  0.0 32.4 jit_solution(5256236799375344754)
XLA Ops:
  0.6 29.6 %fock_build.1.both_ref = f32[2,16,256]{2,1,0:T(8,128)} custom-call(bf16[16,256]{1,0:T(8,128)(2,1)} %density_hbm.1, f32[3,128,128]{2,1,0:T(8,128)} %metric_hbm.1, s32[1,352]{1,0:T(1,128)} %bitcast.3, s32[352]{0:T(512)} %slot_hbm.1, s32[4,2,64]{2,1,0:T(2,128)} %bitcast.2, f32[4,128]{1,0:T(4,128)} %base_rho_hbm.1, f32[4,128]{1,0:T(4,128)} %base_tau_hbm.1, ...), custom_call_target="tpu_custom_call" | custom-call | tf_op jit(solution)/shard_map/fock_build/pallas_call | solution.py:403
  30.3 2.1 %outputs.1 = (f32[16,256]{1,0:T(8,128)}, f32[16,256]{1,0:T(8,128)}) custom-call(f32[2,16,256]{2,1,0:T(8,128)} %fock_build.1.both_ref), custom_call_target="tpu_custom_call" | custom-call | tf_op jit(solution)/shard_map/outputs/pallas_call | solution.py:463

commit v3 on v2

--- a/solution.py
+++ b/solution.py
@@ -233,22 +233,29 @@
 
     copies[8].wait()
     copies[9].wait()
+    def tile_pair(k):
+        a, r = divmod(k, listed)
+        return jnp.concatenate([three[a, r], three[a, r + 1]], axis=1)
+
+    coul_tiles = coul_tiles.astype(BF16)
+    sources = []
     for a in range(aux):
         source = jnp.zeros((2, 2 * grid), F32)
-        for r in range(0, listed, 2):
-            k = a * listed + r
-            pair = jnp.concatenate([three[a, r], three[a, r + 1]], axis=1)
-            source = source + dot(coul_tiles[k : k + 2].astype(BF16), pair)
-        source = source[0:1, :grid] + source[1:2, grid:]
-        coef = dot_nt(source, metric_ref[a], lax.Precision.HIGHEST)
+        for k in range(a * listed, (a + 1) * listed, 2):
+            source = source + dot(coul_tiles[k : k + 2], tile_pair(k))
+        sources.append(source[0:1, :grid] + source[1:2, grid:])
+    coefs = []
+    for a in range(aux):
+        coef = dot_nt(sources[a], metric_ref[a], lax.Precision.HIGHEST)
         none = jnp.zeros_like(coef)
-        coef = jnp.concatenate(
-            [jnp.concatenate([coef, none], axis=1), jnp.concatenate([none, coef], axis=1)], axis=0
-        ).astype(BF16)
-        for r in range(0, listed, 2):
-            k = a * listed + r
-            pair = jnp.concatenate([three[a, r], three[a, r + 1]], axis=1)
-            coul_rows_s[k : k + 2, :] = dot_nt(coef, pair)
+        coefs.append(
+            jnp.concatenate(
+                [jnp.concatenate([coef, none], axis=1), jnp.concatenate([none, coef], axis=1)],
+                axis=0,
+            ).astype(BF16)
+        )
+    for k in range(0, coul_rows, 2):
+        coul_rows_s[k : k + 2, :] = dot_nt(coefs[k // listed], tile_pair(k))
     part = coul_rows_s[...]
     high = part.astype(BF16)
     low = (part - high.astype(F32)).astype(BF16)

time: 32.5 us -> 31.5 us (0.969)
  Pallas kernels: 31.7 us -> 30.7 us
    pallas_call x1, Pallas kernels: 29.6 us -> 28.6 us  [body(): pl.pallas_call(functools.partial(kernel, sizes), out_shape=jax.ShapeDtype...]
where the time goes in v3:
time: 31.5 us; the launch traced here: 31.4 us
  Pallas kernels  30.7 us (97%)
  between operations  0.64 us (2%)
    pallas_call x1, Pallas kernels, body(): pl.pallas_call(functools.partial(kernel, sizes), out_shape=jax.ShapeDtype...  28.6 us
    pallas_call x1, Pallas kernels, body(): pl.pallas_call(part_outputs, out_shape=(out, out), in_specs=[far], out_sp...  2.11 us

profile of v3, /device:TPU:0, one launch (start us, length us, event | category | flops | bytes accessed | tf_op | source)
XLA Modules:
  0.0 31.4 jit_solution(1710112668926304911)
XLA Ops:
  0.6 28.6 %fock_build.1.both_ref = f32[2,16,256]{2,1,0:T(8,128)} custom-call(bf16[16,256]{1,0:T(8,128)(2,1)} %density_hbm.1, f32[3,128,128]{2,1,0:T(8,128)} %metric_hbm.1, s32[1,352]{1,0:T(1,128)} %bitcast.3, s32[352]{0:T(512)} %slot_hbm.1, s32[4,2,64]{2,1,0:T(2,128)} %bitcast.2, f32[4,128]{1,0:T(4,128)} %base_rho_hbm.1, f32[4,128]{1,0:T(4,128)} %base_tau_hbm.1, ...), custom_call_target="tpu_custom_call" | custom-call | tf_op jit(solution)/shard_map/fock_build/pallas_call | solution.py:410
  29.2 2.1 %outputs.1 = (f32[16,256]{1,0:T(8,128)}, f32[16,256]{1,0:T(8,128)}) custom-call(f32[2,16,256]{2,1,0:T(8,128)} %fock_build.1.both_ref), custom_call_target="tpu_custom_call" | custom-call | tf_op jit(solution)/shard_map/outputs/pallas_call | solution.py:470
